TPU v7x, 512 devices: a whole 4x8x8 slice. The times are simulated.
512 devices in a mesh: dom: 32 (over y, x), ref: 16 (over z, core).
Axes of the slice: x: 4, y: 8, z: 8, core: 2. Of those that a mesh axis runs over, the one named last changes fastest.
Arguments:
- particles: bfloat16 [2, 4096, 8192], P(None, ('dom', 'ref')), may hold values from -512 to 512
- defocus: bfloat16 [4096], P(('dom', 'ref')), may hold values from 20 to 60
- references: bfloat16 [2, 512, 8192], P(None, 'ref'), may hold values from -5 to 5
- noise_weights: float32 [8192], replicated, may hold values from 0.005 to 0.05
Outputs:
- updated: float32 [2, 512, 8192], P(None, 'ref', 'dom')
All inputs are finite; a program needn't handle non-finite values.
Results may differ from a plain program's by a relative error of at most 0.0065.
Values may be sent and summed in bfloat16 or wider, within the bound.
A program may use at most 64 MiB of HBM per device.

v0:
```python
import math

import jax
import jax.numpy as jnp
from jax import lax
from jax.sharding import PartitionSpec as P

EDGE = 128
PIX = 8192
TRANS = 4


CONTRAST_SIN = 0.995
CONTRAST_COS = 0.1
SHIFT_PIXELS = 2.0
REGULARIZER = 0.05


def frequencies():
    half_edge = EDGE // 2
    pixel_index = jnp.arange(PIX, dtype=jnp.int32)
    freq_x = (pixel_index // half_edge - half_edge).astype(jnp.float32)
    freq_y = (pixel_index % half_edge).astype(jnp.float32)
    return (freq_x, freq_y)


def contrast(focus, freq_x, freq_y):
    half_edge = EDGE // 2
    radius_sq = (freq_x * freq_x + freq_y * freq_y) / float(half_edge * half_edge)
    phases = focus.astype(jnp.float32)[:, None] * radius_sq[None, :]
    return -(CONTRAST_SIN * jnp.sin(phases) + CONTRAST_COS * jnp.cos(phases))


def weighting(images, focus, noise_weights, freq_x, freq_y):
    transfer = contrast(focus, freq_x, freq_y)
    factor = noise_weights[None, :] * transfer
    weighted = (images.astype(jnp.float32) * factor[None]).astype(jnp.bfloat16)
    ctf_weight = (factor * transfer).astype(jnp.bfloat16)
    return (weighted, ctf_weight)


def shift_tables(freq_x, freq_y):
    shift_ids = jnp.arange(TRANS, dtype=jnp.int32)
    move_x = SHIFT_PIXELS * (shift_ids % 2).astype(jnp.float32)
    move_y = SHIFT_PIXELS * (shift_ids // 2).astype(jnp.float32)
    angles = (
        2.0
        * math.pi
        * (move_x[:, None] * freq_x[None, :] + move_y[:, None] * freq_y[None, :])
        / float(EDGE)
    )
    return (jnp.cos(angles), jnp.sin(angles))


def shifted_references(references, cos_table, sin_table):
    ref_real = references[0].astype(jnp.float32)
    ref_imag = references[1].astype(jnp.float32)
    real_part = ref_real[None] * cos_table[:, None, :] - ref_imag[None] * sin_table[:, None, :]
    imag_part = ref_real[None] * sin_table[:, None, :] + ref_imag[None] * cos_table[:, None, :]
    ref_count = references.shape[1]
    shifted = (
        jnp.stack([real_part, imag_part]).reshape(2, TRANS * ref_count, -1).astype(jnp.bfloat16)
    )
    power = (ref_real * ref_real + ref_imag * ref_imag).astype(jnp.bfloat16)
    return (shifted, power)


def score_rows(weighted, ctf_weight, shifted, power):
    cross_term = jnp.einsum("cnp,cmp->nm", weighted, shifted, preferred_element_type=jnp.float32)
    ctf_term = jnp.einsum("np,mp->nm", ctf_weight, power, preferred_element_type=jnp.float32)
    return cross_term - 0.5 * jnp.tile(ctf_term, (1, TRANS))


def accumulate(running, posterior, occupancy, weighted, ctf_weight, cos_table, sin_table):
    ref_count = occupancy.shape[1]
    image_sums, ctf_sums = running
    for shift_index in range(TRANS):
        columns = posterior[:, shift_index * ref_count : (shift_index + 1) * ref_count]
        per_shift = jnp.einsum("nm,cnp->cmp", columns, weighted, preferred_element_type=jnp.float32)
        real_sum = per_shift[0] * cos_table[shift_index] + per_shift[1] * sin_table[shift_index]
        imag_sum = per_shift[1] * cos_table[shift_index] - per_shift[0] * sin_table[shift_index]
        image_sums = image_sums + jnp.stack([real_sum, imag_sum])
    ctf_sums = jnp.einsum("nm,np->mp", occupancy, ctf_weight, preferred_element_type=jnp.float32)
    return (image_sums, ctf_sums)


def shards(particles, defocus, references, noise_weights):
    freq_x, freq_y = frequencies()
    cos_table, sin_table = shift_tables(freq_x, freq_y)
    shifted, power = shifted_references(references, cos_table, sin_table)
    ref_count = references.shape[1]
    pixels = references.shape[2]
    block_rows = particles.shape[1] * lax.axis_size("ref")
    gathered, block_focus = (
        lax.all_gather(particles, "ref", axis=1, tiled=True),
        lax.all_gather(defocus, "ref", axis=0, tiled=True),
    )
    weighted, ctf_weight = weighting(gathered, block_focus, noise_weights, freq_x, freq_y)
    scores = score_rows(weighted, ctf_weight, shifted, power)
    row_top = jnp.max(scores, axis=1)
    row_top = lax.pmax(row_top, "ref")
    row_sum = lax.psum(jnp.sum(jnp.exp(scores - row_top[:, None]), axis=1), "ref")
    log_norm = row_top + jnp.log(row_sum)
    posterior = jnp.exp(scores - log_norm[:, None]).astype(jnp.bfloat16)
    occupancy = jnp.sum(
        posterior.astype(jnp.float32).reshape(block_rows, TRANS, ref_count), axis=1
    ).astype(jnp.bfloat16)
    empty = (
        jnp.zeros((2, ref_count, pixels), jnp.float32),
        jnp.zeros((ref_count, pixels), jnp.float32),
    )
    image_sums, ctf_sums = accumulate(
        empty, posterior, occupancy, weighted, ctf_weight, cos_table, sin_table
    )
    image_part, ctf_part = (
        lax.psum_scatter(image_sums, "dom", scatter_dimension=2, tiled=True),
        lax.psum_scatter(ctf_sums, "dom", scatter_dimension=1, tiled=True),
    )
    return image_part / (ctf_part[None] + REGULARIZER)


def solution(mesh):
    return jax.shard_map(
        shards,
        mesh=mesh,
        in_specs=(P(None, ("dom", "ref"), None), P(("dom", "ref")), P(None, "ref", None), P()),
        out_specs=P(None, "ref", "dom"),
        check_vma=False,
    )
```

profile of v0, /device:TPU:16, one launch (start us, length us, event | category | flops | bytes accessed | tf_op | source)
XLA Modules:
  0.0 608.6 jit_solution(2680301421486855027)
XLA Ops:
  6.5 0.0 all-gather.2.cloned.1.call-start
  6.5 0.7 all-gather.2.cloned.1.call-update
  7.3 0.0 reduce-scatter.5.cloned.1.call-start
  7.4 1.3 dynamic-slice
  9.3 0.9 dynamic-update-slice
  10.2 32.2 %all-reduce = bf16[128]{0:T(256)(128)(2,1)S(1)} all-reduce(bf16[128]{0:T(256)(128)(2,1)S(1)} %dynamic-update-slice), channel_id=1, replica_groups=mesh['dom'=32,'ref'=16] {'ref'}, use_global_device_ids=true, to_apply=%add | all-reduce | flops 128 | bytes 512
  42.4 1.1 fusion.29
  43.5 0.0 copy-start.5
  43.5 0.0 copy-start.6
  43.5 17.7 %convolution_multiply_fusion = f32[128,32]{0,1:T(8,128)S(1)} fusion(f32[8192]{0:T(1024)S(1)} %add_multiply_fusion.1, f32[128]{0:T(128)S(1)} %convert_element_type.227, f32[8192]{0:T(1024)} %param.7, bf16[2,32,8192]{2,1,0:T(8,128)(2,1)} %param.6), kind=kOutput, calls=%fused_computation.29 | convolution fusion | flops 77074432 | bytes 1131008 | tf_op jit(solution)/shard_map/np,mp->nm/dot_general | solution.py:70
  61.3 0.2 fusion.49
  61.4 0.0 copy-done.5
  61.5 0.1 convert_bitcast_fusion.1
  61.6 0.0 copy-done.6
  61.6 16.5 %fusion.5 = f32[128,8192]{1,0:T(8,128)} fusion(f32[8192]{0:T(1024)S(1)} %add_multiply_fusion.1, f32[128]{0:T(128)S(1)} %convert_element_type.227, f32[8192]{0:T(1024)S(1)} %copy-done.6), kind=kLoop, calls=%fused_computation.12 | loop fusion | flops 6291456 | bytes 4260352 | tf_op jit(solution)/shard_map/mul | solution.py:36
  78.1 2.4 subtract_convert_fusion
  80.5 0.0 all-gather.2.cloned.1.call-done
  80.5 0.0 copy-start.4
  80.5 4.6 multiply_convert_fusion
  85.1 0.0 copy-start
  85.1 0.0 copy-done.4
  85.2 1.3 fusion.51
  86.4 0.6 copy-done
  87.1 23.5 %pmax.7 = f32[128]{0:T(128)S(1)} all-reduce(f32[128]{0:T(128)S(1)} %get-tuple-element.27), channel_id=1, replica_groups=mesh['dom'=32,'ref'=16] {'ref'}, use_global_device_ids=true, to_apply=%region_1.2 | all-reduce | flops 128 | bytes 1024 | tf_op jit(solution)/shard_map/pmax | solution.py:101
  110.6 23.7 %psum.7 = f32[128]{0:T(128)S(1)} all-reduce(f32[128]{0:T(128)S(1)} %exponential_reduce_fusion), channel_id=1, replica_groups=mesh['dom'=32,'ref'=16] {'ref'}, use_global_device_ids=true, to_apply=%region_3.4 | all-reduce | flops 128 | bytes 1024 | tf_op jit(solution)/shard_map/psum | solution.py:102
  134.4 0.0 copy-start.1
  134.4 4.3 convolution_bitcast_fusion
  138.7 0.0 copy-done.1
  138.7 2.0 convolution_bitcast_fusion.1
  140.7 2.0 convolution_bitcast_fusion.2
  142.8 0.7 convolution_bitcast_fusion.3
  143.5 16.6 %fusion.19 = f32[32,8192]{1,0:T(8,128)} fusion(bf16[128,32]{0,1:T(8,128)(2,1)S(1)} %reduce, f32[8192]{0:T(1024)S(1)} %add_multiply_fusion.1, f32[128]{0:T(128)S(1)} %convert_element_type.227, f32[8192]{0:T(1024)S(1)} %copy-done.6), kind=kOutput, calls=%fused_computation.30 | convolution fusion | flops 75497472 | bytes 1122816 | tf_op jit(solution)/shard_map/nm,np->mp/dot_general | solution.py:83
  160.0 0.0 reduce-scatter.5.cloned.1.call-update
  160.1 0.0 reduce-scatter.3.cloned.1.call-start
  160.1 0.0 copy-start.3
  160.1 0.0 copy-start.2
  160.1 1.9 multiply_add_fusion
  162.1 0.3 copy-done.3
  162.3 0.2 multiply_add_fusion.1
  162.6 0.4 copy-done.2
  163.0 0.2 multiply_add_fusion.2
  163.2 0.2 multiply_add_fusion.3
  163.5 1.8 fusion.12
  165.2 0.0 reduce-scatter.3.cloned.1.call-update
  165.2 210.8 %reduce-scatter.5.cloned.1.call-done = f32[32,256]{1,0:T(8,128)} async-done(((f32[32,8192]{1,0:T(8,128)}), f32[32,256]{1,0:T(8,128)}) %reduce-scatter.5.cloned.1.call-update) | async-done | bytes 32784 | tf_op jit(solution)/shard_map/reduce_scatter | solution.py:117
  376.0 0.8 broadcast_add_fusion
  376.8 223.7 %reduce-scatter.3.cloned.1.call-done = f32[2,32,256]{2,1,0:T(8,128)} async-done(((f32[2,32,8192]{2,1,0:T(8,128)}), f32[2,32,256]{2,1,0:T(8,128)}) %reduce-scatter.3.cloned.1.call-update) | async-done | bytes 65552 | tf_op jit(solution)/shard_map/reduce_scatter | solution.py:116
  600.5 1.5 broadcast_divide_fusion
  (12 shorter events, 0.1 us)
Async XLA Ops:
  6.5 73.9 %all-gather.2.cloned.1.call-start = ((), (), s32[]{:S(2)}) async-start(), calls=%async_computation.2 | async-start | bytes 4456448 | tf_op jit(solution)/shard_map/all_gather | solution.py:95
  7.3 368.7 %reduce-scatter.5.cloned.1.call-start = ((), (), s32[]{:S(2)}) async-start(), calls=%async_computation.4 | async-start | bytes 1081344 | tf_op jit(solution)/shard_map/reduce_scatter | solution.py:117
  43.5 18.0 %copy-start.5 = (bf16[2,32,8192]{2,1,0:T(8,128)(2,1)S(1)}, bf16[2,32,8192]{2,1,0:T(8,128)(2,1)}, u32[]{:S(2)}) copy-start(bf16[2,32,8192]{2,1,0:T(8,128)(2,1)} %param.6) | copy-start | bytes 3145732
  43.5 18.1 %copy-start.6 = (f32[8192]{0:T(1024)S(1)}, f32[8192]{0:T(1024)}, u32[]{:S(2)}) copy-start(f32[8192]{0:T(1024)} %param.7) | copy-start | bytes 98308
  80.5 4.7 copy-start.4
  85.1 1.9 copy-start
  134.4 4.4 copy-start.1
  160.1 440.4 %reduce-scatter.3.cloned.1.call-start = ((), (), s32[]{:S(2)}) async-start(), calls=%async_computation.3 | async-start | bytes 2162688 | tf_op jit(solution)/shard_map/reduce_scatter | solution.py:116
  160.1 2.2 copy-start.3
  160.1 2.8 copy-start.2
Sparse Core Ops, SparseCore 0:
  9.5 49.7 all-gather.1
  160.2 215.7 reduce-scatter.4
  380.4 219.9 reduce-scatter.2
where the time goes:
time: 618 us; the launch traced here: 609 us
  waiting for transfers between devices  435 us (70%)
  blocking collectives  79.4 us (13%)
  matrix products  44.6 us (7%)
  other arithmetic  31.5 us (5%)
  between operations  14.2 us (2%)
    reduce_scatter x1, waiting for transfers between devices, shards(): lax.psum_scatter(image_sums, 'dom', scatter_dimension=2, tiled=True)  224 us
    reduce_scatter x1, waiting for transfers between devices, shards(): lax.psum_scatter(ctf_sums, 'dom', scatter_dimension=1, tiled=True)  211 us
    unnamed x1, blocking collectives  32.2 us
    psum x1, blocking collectives, shards(): lax.psum(jnp.sum(jnp.exp(scores - row_top[:, None]), axis=1), 'ref')  23.7 us
    pmax x1, blocking collectives, shards(): row_top = lax.pmax(row_top, 'ref')  23.5 us
    dot_general x1, matrix products, score_rows(): jnp.einsum('np,mp->nm', ctf_weight, power, preferred_element_type=jnp.flo...  17.7 us
    dot_general x1, matrix products, accumulate(): jnp.einsum('nm,np->mp', occupancy, ctf_weight, preferred_element_type=jnp...  16.6 us
    mul x1, other arithmetic, weighting(): factor = noise_weights[None, :] * transfer  16.5 us
  transfers between devices with their start and end apart: 3, of which 2 were waited for; matrix products, arithmetic and copies ran while one was open for 7% of the time, Pallas kernels for 0%

commit v1 on v0

v1 whole, which is shorter than its diff:
```python
import jax
import jax.numpy as jnp
from jax import lax
from jax.experimental import pallas as pl
from jax.experimental.pallas import tpu as pltpu
from jax.sharding import PartitionSpec as P

PIX = 8192
TRANS = 4
REFS = 32
SX, SY, SZ = 4, 8, 8
NCHUNK = 4
CHUNK = PIX // NCHUNK
SLICE = 1024
OUT = 256
REGULARIZER = 0.05

AMP = 1.000012499921876
PHASE = 0.015941940272471127
INV_TWO_PI = 0.15915494309189535
SIN_TERMS = (
    6.283182818554191,
    -41.341421398928475,
    81.5961838781331,
    -76.58010057017961,
    41.205395033387106,
    -12.271262585212861,
)

MESH = pl.DeviceIdType.MESH
F32 = jnp.float32
BF16 = jnp.bfloat16


def sin_turns(turns):
    v = turns - jnp.round(turns)
    sq = v * v
    acc = sq * SIN_TERMS[5] + SIN_TERMS[4]
    for term in SIN_TERMS[3::-1]:
        acc = acc * sq + term
    return acc * v


def nt_dot(a, b):
    return lax.dot_general(a, b, (((1,), (1,)), ((), ())), preferred_element_type=F32)


def twice(a):
    return jnp.concatenate([a, a], axis=0)


def kernel(
    part_ref, focus_ref, refs_ref, noise_ref, out_ref,
    gath, focus, tab, factor, wgt, cwt, shf, pwr, score, cterm, stat, post, occ,
    xsend, xrecv, ysend, yrecv, own_sum,
    local_sem, ring_send, ring_recv, core_send, core_recv,
    fsend, frecv, ssend, srecv, xs_sem, xr_sem, ys_sem, yr_sem,
):
    dom, me = lax.axis_index("dom"), lax.axis_index("ref")
    y, x, z, c = dom // SX, dom % SX, me // 2, me % 2
    other = (dom, z * 2 + 1 - c)
    up = (dom, lax.rem(z + 1, SZ) * 2 + c)
    down = (dom, lax.rem(z + SZ - 1, SZ) * 2 + c)

    def mate(step):
        return lax.rem(me + step, 2 * SZ)

    def x_mate(step):
        return (y * SX + lax.rem(x + step, SX), me)

    def y_mate(step):
        return (lax.rem(y + step, SY) * SX + x, me)

    barrier = pltpu.get_barrier_semaphore()
    for step in range(1, 2 * SZ):
        pl.semaphore_signal(barrier, inc=1, device_id=(dom, mate(step)), device_id_type=MESH)
    for step in range(1, SX):
        pl.semaphore_signal(barrier, inc=1, device_id=x_mate(step), device_id_type=MESH)
    for step in range(1, SY):
        pl.semaphore_signal(barrier, inc=1, device_id=y_mate(step), device_id_type=MESH)
    own = pltpu.make_async_copy(part_ref, gath.at[me], local_sem)
    own.start()
    focus[me] = focus_ref[...]
    own.wait()
    pl.semaphore_wait(barrier, 2 * SZ - 1 + SX - 1 + SY - 1)

    def cols(j):
        return pl.ds(pl.multiple_of(j * CHUNK, CHUNK), CHUNK)

    def ring_copy(way, step, j):
        block = lax.rem(z + SZ - step, SZ) if way == 0 else lax.rem(z + step, SZ)
        ref = gath.at[block * 2 + c, :, cols(j)]
        return pltpu.make_async_remote_copy(
            ref, ref, ring_send.at[way, step, j], ring_recv.at[way, step, j],
            device_id=up if way == 0 else down, device_id_type=MESH,
        )

    def ring_landed(way, step, j):
        block = lax.rem(z + 2 * SZ - step - 1, SZ) if way == 0 else lax.rem(z + step + 1, SZ)
        ref = gath.at[block * 2 + c, :, cols(j)]
        pltpu.make_async_remote_copy(
            ref, ref, ring_send.at[way, step, j], ring_recv.at[way, step, j],
            device_id=up if way == 0 else down, device_id_type=MESH,
        ).wait_recv()

    def core_copy(dist, j):
        ref = gath.at[lax.rem(z + dist, SZ) * 2 + c, :, cols(j)]
        return pltpu.make_async_remote_copy(
            ref, ref, core_send.at[dist, j], core_recv.at[dist, j],
            device_id=other, device_id_type=MESH,
        )

    def core_landed(dist, j):
        ref = gath.at[lax.rem(z + dist, SZ) * 2 + 1 - c, :, cols(j)]
        pltpu.make_async_remote_copy(
            ref, ref, core_send.at[dist, j], core_recv.at[dist, j],
            device_id=other, device_id_type=MESH,
        ).wait_recv()

    def focus_copy(step):
        return pltpu.make_async_remote_copy(
            focus.at[me], focus.at[me], fsend.at[step - 1], frecv.at[step - 1],
            device_id=(dom, mate(step)), device_id_type=MESH,
        )

    def focus_landed(step):
        ref = focus.at[lax.rem(me + 2 * SZ - step, 2 * SZ)]
        pltpu.make_async_remote_copy(
            ref, ref, fsend.at[step - 1], frecv.at[step - 1],
            device_id=(dom, mate(step)), device_id_type=MESH,
        ).wait_recv()

    def stat_copy(step):
        return pltpu.make_async_remote_copy(
            stat.at[me], stat.at[me], ssend.at[step - 1], srecv.at[step - 1],
            device_id=(dom, mate(step)), device_id_type=MESH,
        )

    def stat_landed(step):
        ref = stat.at[lax.rem(me + 2 * SZ - step, 2 * SZ)]
        pltpu.make_async_remote_copy(
            ref, ref, ssend.at[step - 1], srecv.at[step - 1],
            device_id=(dom, mate(step)), device_id_type=MESH,
        ).wait_recv()

    for j in range(NCHUNK):
        ring_copy(0, 0, j).start()
        ring_copy(1, 0, j).start()
    for step in range(1, 2 * SZ):
        focus_copy(step).start()
    for j in range(NCHUNK):
        core_copy(0, j).start()

    def tables_and_shifts(k):
        at = pl.ds(pl.multiple_of(k * SLICE, SLICE), SLICE)
        pixel = lax.broadcasted_iota(jnp.int32, (8, SLICE), 1) + k * SLICE
        fx = (lax.shift_right_logical(pixel, 6) - 64).astype(F32)
        fy = (pixel & 63).astype(F32)
        tab[0, :, at] = (fx * fx + fy * fy) * (INV_TWO_PI / 4096.0)
        trig = []
        for turns in (fx * (1.0 / 64.0), fy * (1.0 / 64.0), (fx + fy) * (1.0 / 64.0)):
            cos, sin = sin_turns(turns + 0.25), sin_turns(turns)
            trig.append((cos, sin))
        for t, (cos, sin) in enumerate(trig):
            tab[1 + 2 * t, :, at] = cos
            tab[2 + 2 * t, :, at] = sin
        for half in range(REFS // 16):
            rows = slice(16 * half, 16 * half + 16)
            real, imag = refs_ref[0, rows, at], refs_ref[1, rows, at]
            shf[0, rows, at] = real
            shf[1, rows, at] = imag
            real, imag = real.astype(F32), imag.astype(F32)
            power = (real * real + imag * imag).astype(BF16)
            for t in range(TRANS):
                to = slice(t * REFS + 16 * half, t * REFS + 16 * half + 16)
                pwr[to, at] = power
                if t:
                    cos, sin = twice(trig[t - 1][0]), twice(trig[t - 1][1])
                    shf[0, to, at] = (real * cos - imag * sin).astype(BF16)
                    shf[1, to, at] = (real * sin + imag * cos).astype(BF16)

    def contrast(k):
        at = pl.ds(pl.multiple_of(k * SLICE, SLICE), SLICE)

        def rows16(i, _):
            rows = pl.ds(pl.multiple_of(i * 16, 16), 16)
            turns = twice(tab[0, :, at])
            d0, d1 = focus[2 * i], focus[2 * i + 1]
            d = jnp.concatenate([d0, d1], axis=0)[:, :1]
            transfer = sin_turns(turns * d + PHASE) * (-AMP)
            fac = transfer * noise_ref[:, at]
            factor[rows, at] = fac
            cwt[rows, at] = (fac * transfer).astype(BF16)
            return 0

        lax.fori_loop(0, SZ, rows16, 0)
        cterm[...] += nt_dot(pwr[:, at], cwt[:, at])

    def events(e, j_all):
        del j_all
        step, j = e // NCHUNK, lax.rem(e, NCHUNK)
        for s in range(SZ // 2):

            @pl.when(step == s)
            def _():
                if s < 3:
                    for way in range(2):
                        ring_landed(way, s, j)
                    if s < 2:
                        for way in range(2):
                            ring_copy(way, s + 1, j).start()
                    else:

                        @pl.when(j < 2)
                        def _():
                            ring_copy(0, 3, j).start()

                        @pl.when(j >= 2)
                        def _():
                            ring_copy(1, 3, j).start()

                    core_copy(SZ - 1 - s, j).start()
                    core_copy(s + 1, j).start()
                else:

                    @pl.when(j < 2)
                    def _():
                        ring_landed(0, 3, j)

                    @pl.when(j >= 2)
                    def _():
                        ring_landed(1, 3, j)

                    core_copy(4, j).start()

    cterm[...] = jnp.zeros_like(cterm)

    def first(e, _):
        tables_and_shifts(e)
        events(e, None)
        return 0

    lax.fori_loop(0, 8, first, 0)
    for step in range(1, 2 * SZ):
        focus_landed(step)

    def second(e, _):
        contrast(2 * e)
        contrast(2 * e + 1)
        events(e + 8, None)
        return 0

    lax.fori_loop(0, 4, second, 0)

    score[...] = jnp.zeros_like(score)

    def third(j, _):
        events(j + 12, None)
        at = cols(j)
        for dist in range(SZ):
            core_landed(dist, j)

        def weigh(i, _):
            rows = pl.ds(pl.multiple_of(i * 16, 16), 16)
            fac = factor[rows, at]
            a = gath[2 * i, :, at].astype(F32)
            b = gath[2 * i + 1, :, at].astype(F32)
            for comp in range(2):
                pick = slice(8 * comp, 8 * comp + 8)
                wgt[comp, rows, at] = (
                    jnp.concatenate([a[pick], b[pick]], axis=0) * fac
                ).astype(BF16)
            return 0

        lax.fori_loop(0, SZ, weigh, 0)
        score[...] += nt_dot(shf[0, :, at], wgt[0, :, at]) + nt_dot(shf[1, :, at], wgt[1, :, at])
        return 0

    lax.fori_loop(0, NCHUNK, third, 0)

    scores = score[...] - 0.5 * cterm[...]
    top = jnp.max(scores, axis=0, keepdims=True)
    total = jnp.sum(jnp.exp(scores - top), axis=0, keepdims=True)
    stat[me] = jnp.concatenate([top, total, jnp.zeros((6, 128), F32)], axis=0)
    for step in range(1, 2 * SZ):
        stat_copy(step).start()
    score[...] = scores
    for step in range(1, 2 * SZ):
        stat_landed(step)
    stats = stat[...]
    tops, totals = stats[:, 0, :], stats[:, 1, :]
    all_top = jnp.max(tops, axis=0, keepdims=True)
    all_total = jnp.sum(totals * jnp.exp(tops - all_top), axis=0, keepdims=True)
    log_norm = all_top + jnp.log(all_total)
    posterior = jnp.exp(score[...] - log_norm).astype(BF16)
    post[...] = posterior
    wide = posterior.astype(F32)
    occ[...] = (
        wide[0:REFS] + wide[REFS : 2 * REFS] + wide[2 * REFS : 3 * REFS] + wide[3 * REFS :]
    ).astype(BF16)

    def y_step(i):
        return 4 + (1 - 2 * lax.rem(i, 2)) * ((i + 1) // 2)

    def x_copy(i, step):
        return pltpu.make_async_remote_copy(
            xsend.at[i, lax.rem(x + step, SX)], xrecv.at[i, step - 1],
            xs_sem.at[i, step - 1], xr_sem.at[i, step - 1],
            device_id=x_mate(step), device_id_type=MESH,
        )

    def y_copy(i):
        step = y_step(i)
        return pltpu.make_async_remote_copy(
            ysend.at[i], yrecv.at[i], ys_sem.at[i], yr_sem.at[i],
            device_id=y_mate(step), device_id_type=MESH,
        )

    def piece(i, _):
        base = lax.rem(y + y_step(i), SY) * SLICE

        def quarter(q, _):
            at = pl.ds(pl.multiple_of(base + q * OUT, OUT), OUT)
            a0 = jnp.dot(post[...], wgt[0, :, at], preferred_element_type=F32)
            a1 = jnp.dot(post[...], wgt[1, :, at], preferred_element_type=F32)
            ctf = jnp.dot(occ[...], cwt[:, at], preferred_element_type=F32)
            real, imag = a0[0:REFS], a1[0:REFS]
            for t in range(1, TRANS):
                cos, sin = tab[2 * t - 1, :, at], tab[2 * t, :, at]
                cos = jnp.concatenate([cos] * (REFS // 8), axis=0)
                sin = jnp.concatenate([sin] * (REFS // 8), axis=0)
                b0, b1 = a0[t * REFS : (t + 1) * REFS], a1[t * REFS : (t + 1) * REFS]
                real = real + b0 * cos + b1 * sin
                imag = imag + b1 * cos - b0 * sin
            xsend[i, q, 0:REFS] = real.astype(BF16)
            xsend[i, q, REFS : 2 * REFS] = imag.astype(BF16)
            xsend[i, q, 2 * REFS :] = ctf.astype(BF16)
            return 0

        lax.fori_loop(0, SX, quarter, 0)
        for step in range(1, SX):
            x_copy(i, step).start()
        return 0

    lax.fori_loop(0, SY, piece, 0)

    def x_total(i):
        for step in range(1, SX):
            x_copy(i, step).wait_recv()
        acc = xsend[i, x].astype(F32)
        for step in range(1, SX):
            acc = acc + xrecv[i, step - 1].astype(F32)
        return acc

    def forward(i, _):
        ysend[i] = x_total(i).astype(BF16)
        y_copy(i).start()
        return 0

    lax.fori_loop(0, SY - 1, forward, 0)
    own_sum[...] = x_total(SY - 1)

    def collect(i, _):
        y_copy(i).wait_recv()
        own_sum[...] += yrecv[i].astype(F32)
        return 0

    lax.fori_loop(0, SY - 1, collect, 0)
    weight = own_sum[2 * REFS :] + REGULARIZER
    out_ref[0] = own_sum[0:REFS] / weight
    out_ref[1] = own_sum[REFS : 2 * REFS] / weight

    def drain_ring(e, _):
        j = lax.rem(e, NCHUNK)
        for s in range(SZ // 2):

            @pl.when(e // NCHUNK == s)
            def _():
                if s < 3:
                    ring_copy(0, s, j).wait_send()
                    ring_copy(1, s, j).wait_send()
                else:

                    @pl.when(j < 2)
                    def _():
                        ring_copy(0, 3, j).wait_send()

                    @pl.when(j >= 2)
                    def _():
                        ring_copy(1, 3, j).wait_send()

        return 0

    lax.fori_loop(0, 16, drain_ring, 0)

    def drain_core(dist, _):
        for j in range(NCHUNK):
            core_copy(dist, j).wait_send()
        return 0

    lax.fori_loop(0, SZ, drain_core, 0)

    def drain_mates(step, _):
        focus_copy(step).wait_send()
        stat_copy(step).wait_send()
        return 0

    lax.fori_loop(1, 2 * SZ, drain_mates, 0)

    def drain_sums(i, _):
        for step in range(1, SX):
            x_copy(i, step).wait_send()
        return 0

    lax.fori_loop(0, SY, drain_sums, 0)

    def drain_y(i, _):
        y_copy(i).wait_send()
        return 0

    lax.fori_loop(0, SY - 1, drain_y, 0)


def shards(particles, defocus, references, noise_weights):
    dma = pltpu.SemaphoreType.DMA
    nref = TRANS * REFS
    nblock = 2 * SZ
    rows = particles.shape[0] * particles.shape[1]
    focus = jnp.broadcast_to(defocus.astype(F32)[:, None], (8, 128))
    vmem = pl.BlockSpec(memory_space=pltpu.VMEM)
    return pl.pallas_call(
        kernel,
        out_shape=jax.ShapeDtypeStruct((2, REFS, OUT), F32),
        in_specs=[pl.BlockSpec(memory_space=pl.ANY), vmem, vmem, vmem],
        out_specs=vmem,
        scratch_shapes=[
            pltpu.VMEM((nblock, rows, PIX), BF16),
            pltpu.VMEM((nblock, 8, 128), F32),
            pltpu.VMEM((7, 8, PIX), F32),
            pltpu.VMEM((128, PIX), F32),
            pltpu.VMEM((2, 128, PIX), BF16),
            pltpu.VMEM((128, PIX), BF16),
            pltpu.VMEM((2, nref, PIX), BF16),
            pltpu.VMEM((nref, PIX), BF16),
            pltpu.VMEM((nref, 128), F32),
            pltpu.VMEM((nref, 128), F32),
            pltpu.VMEM((nblock, 8, 128), F32),
            pltpu.VMEM((nref, 128), BF16),
            pltpu.VMEM((REFS, 128), BF16),
            pltpu.VMEM((SY, SX, 3 * REFS, OUT), BF16),
            pltpu.VMEM((SY, SX - 1, 3 * REFS, OUT), BF16),
            pltpu.VMEM((SY - 1, 3 * REFS, OUT), BF16),
            pltpu.VMEM((SY - 1, 3 * REFS, OUT), BF16),
            pltpu.VMEM((3 * REFS, OUT), F32),
            dma,
            dma((2, 4, NCHUNK)),
            dma((2, 4, NCHUNK)),
            dma((SZ, NCHUNK)),
            dma((SZ, NCHUNK)),
            dma((nblock - 1,)),
            dma((nblock - 1,)),
            dma((nblock - 1,)),
            dma((nblock - 1,)),
            dma((SY, SX - 1)),
            dma((SY, SX - 1)),
            dma((SY - 1,)),
            dma((SY - 1,)),
        ],
        name="expectation",
        compiler_params=pltpu.CompilerParams(
            collective_id=0, has_side_effects=True, vmem_limit_bytes=56 * 2**20
        ),
    )(particles.reshape(rows, PIX), focus, references, noise_weights.reshape(1, PIX))


def solution(mesh):
    return jax.shard_map(
        shards,
        mesh=mesh,
        in_specs=(P(None, ("dom", "ref"), None), P(("dom", "ref")), P(None, "ref", None), P()),
        out_specs=P(None, "ref", "dom"),
        check_vma=False,
    )
```

time: 618 us -> 82.1 us (0.13)
  the two profiles are of different devices: /device:TPU:16 before, /device:TPU:1 now
where the time goes in v1:
time: 82.1 us; the launch traced here: 80.6 us
  Pallas kernels  77.8 us (95%)
  local copies, waits for them, and re-layouts  2.79 us (3%)
    pallas_call x1, Pallas kernels, shards(): pl.pallas_call(kernel, out_shape=jax.ShapeDtypeStruct((2, REFS, OUT), F32...  77.8 us
    unnamed x3, local copies, waits for them, and re-layouts  2.13 us

profile of v1, /device:TPU:1, one launch (start us, length us, event | category | flops | bytes accessed | tf_op | source)
XLA Modules:
  0.0 80.6 jit_solution(1262014490605961855)
XLA Ops:
  0.0 0.0 copy-start
  0.0 0.7 copy-done
  0.7 0.7 broadcast_in_dim.2.focus_ref
  1.3 77.8 %expectation.1 = f32[2,32,256]{2,1,0:T(8,128)} custom-call(bf16[16,8192]{1,0:T(8,128)(2,1)} %bitcast.2, f32[8,128]{1,0:T(8,128)} %broadcast_in_dim.2.focus_ref, bf16[2,32,8192]{2,1,0:T(8,128)(2,1)} %refs_ref.1, f32[1,8192]{1,0:T(1,128)} %bitcast.3), custom_call_target="tpu_custom_call" | custom-call | tf_op jit(solution)/shard_map/expectation/pallas_call | solution.py:431
  79.1 1.5 %copy.6 = f32[2,32,256]{2,1,0:T(8,128)} copy(f32[2,32,256]{2,1,0:T(8,128)} %expectation.1) | data formatting | bytes 131072
Async XLA Ops:
  0.0 0.7 copy-start

commit v2 on v0

v2 whole, which is shorter than its diff:
```python
import jax
import jax.numpy as jnp
from jax import lax
from jax.experimental import pallas as pl
from jax.experimental.pallas import tpu as pltpu
from jax.sharding import PartitionSpec as P

PIX = 8192
TRANS = 4
REFS = 32
SX, SY, SZ = 4, 8, 8
OUT = 256
ROW = SX * OUT
LOCAL = SY * OUT
WIDE = LOCAL + 128
PART = 512
HALF = SX // 2
NREF = TRANS * REFS
NPART = SZ * SX * 16
REGULARIZER = 0.05

AMP = 1.000012499921876
PHASE = 0.015941940272471127
INV_TWO_PI = 0.15915494309189535
SIN_TERMS = (
    6.283182818554191,
    -41.341421398928475,
    81.5961838781331,
    -76.58010057017961,
    41.205395033387106,
    -12.271262585212861,
)

MESH = pl.DeviceIdType.MESH
F32 = jnp.float32
BF16 = jnp.bfloat16


def sin_turns(turns):
    v = turns - jnp.round(turns)
    sq = v * v
    acc = sq * SIN_TERMS[5] + SIN_TERMS[4]
    for term in SIN_TERMS[3::-1]:
        acc = acc * sq + term
    return acc * v


def nt_dot(a, b):
    return lax.dot_general(a, b, (((1,), (1,)), ((), ())), preferred_element_type=F32)


def twice(a):
    return jnp.concatenate([a, a], axis=0)


def kernel(
    part_ref, focus_ref, refs_ref, noise_ref, out_ref,
    gath, focus, refs, tab, wgt, shf, score, stat, flip, post, occ, ysend, yrecv, total,
    local_sem, refs_sem, asend, arecv, ring_send, ring_recv, core_send, core_recv,
    tsend, trecv, ssend, srecv, ys_sem, yr_sem,
):
    dom, me = lax.axis_index("dom"), lax.axis_index("ref")
    y, x, z, c = dom // SX, dom % SX, me // 2, me % 2
    other = (dom, z * 2 + 1 - c)
    up = (dom, lax.rem(z + 1, SZ) * 2 + c)
    down = (dom, lax.rem(z + SZ - 1, SZ) * 2 + c)

    def remote(src, dst, send, recv, device):
        return pltpu.make_async_remote_copy(
            src, dst, send, recv, device_id=device, device_id_type=MESH
        )

    def mate(step):
        return (dom, lax.rem(me + step, 2 * SZ))

    def x_mate(step):
        return (y * SX + lax.rem(x + step, SX), me)

    def y_mate(step):
        return (lax.rem(y + step, SY) * SX + x, me)

    def source(o):
        return lax.rem(x + SX - o, SX)

    def strip(q, to):
        return pl.ds(pl.multiple_of(q * ROW + to * OUT, OUT), OUT)

    def local(q):
        return pl.ds(pl.multiple_of(q * OUT, OUT), OUT)

    barrier = pltpu.get_barrier_semaphore()
    for step in range(1, 2 * SZ):
        pl.semaphore_signal(barrier, inc=1, device_id=mate(step), device_id_type=MESH)
    for step in range(1, SX):
        pl.semaphore_signal(barrier, inc=1, device_id=x_mate(step), device_id_type=MESH)
    for step in range(1, SY):
        pl.semaphore_signal(barrier, inc=1, device_id=y_mate(step), device_id_type=MESH)

    for q in range(SY):
        pltpu.make_async_copy(
            part_ref.at[:, strip(q, x)], gath.at[me, x, :, local(q)], local_sem
        ).start()
    for q in range(SY):
        pltpu.make_async_copy(
            refs_ref.at[:, :, strip(q, x)], refs.at[:, :, local(q)], refs_sem
        ).start()
    diagonal = lax.broadcasted_iota(jnp.int32, (8, 8), 0) == lax.broadcasted_iota(
        jnp.int32, (8, 8), 1
    )
    wide = jnp.broadcast_to(focus_ref[...].astype(F32), (8, 8))
    column = jnp.sum(jnp.where(diagonal, wide, 0.0), axis=1, keepdims=True)
    spread = twice(jnp.broadcast_to(column, (8, 128))).astype(BF16)
    focus[...] = spread
    gath[me, x, :, LOCAL:] = spread
    here = gath.at[me, x, :, pl.ds(0, LOCAL)]
    pltpu.make_async_copy(here, here, local_sem).wait()
    pl.semaphore_wait(barrier, 2 * SZ - 1 + SX - 1 + SY - 1)

    def ring_copy(way, step, o):
        block = lax.rem(z + SZ - step, SZ) if way == 0 else lax.rem(z + step, SZ)
        ref = gath.at[block * 2 + c, source(o)]
        return remote(
            ref, ref, ring_send.at[way, step, o], ring_recv.at[way, step, o],
            up if way == 0 else down,
        )

    def ring_landed(way, step, o):
        block = lax.rem(z + 2 * SZ - step - 1, SZ) if way == 0 else lax.rem(z + step + 1, SZ)
        ref = gath.at[block * 2 + c, source(o)]
        remote(
            ref, ref, ring_send.at[way, step, o], ring_recv.at[way, step, o],
            up if way == 0 else down,
        ).wait_recv()

    def core_copy(dist, o):
        ref = gath.at[lax.rem(z + dist, SZ) * 2 + c, source(o)]
        return remote(ref, ref, core_send.at[dist, o], core_recv.at[dist, o], other)

    def core_landed(dist, o):
        ref = gath.at[lax.rem(z + dist, SZ) * 2 + 1 - c, source(o)]
        remote(ref, ref, core_send.at[dist, o], core_recv.at[dist, o], other).wait_recv()

    def swap_landed(o):
        ref = gath.at[me, source(o)]
        remote(ref, ref, asend.at[o - 1], arecv.at[o - 1], x_mate(o)).wait_recv()

    def term_copy(dist, o):
        ref = score.at[x, lax.rem(z + dist, SZ)]
        return remote(ref, ref, tsend.at[dist, o - 1], trecv.at[dist, o - 1], x_mate(o))

    def term_landed(dist, o):
        ref = score.at[source(o), lax.rem(z + dist, SZ)]
        remote(ref, ref, tsend.at[dist, o - 1], trecv.at[dist, o - 1], x_mate(o)).wait_recv()

    def stat_copy(step):
        return remote(
            stat.at[me], stat.at[me], ssend.at[step - 1], srecv.at[step - 1], mate(step)
        )

    def stat_landed(step):
        ref = stat.at[lax.rem(me + 2 * SZ - step, 2 * SZ)]
        remote(ref, ref, ssend.at[step - 1], srecv.at[step - 1], mate(step)).wait_recv()

    ring_copy(0, 0, 0).start()
    ring_copy(1, 0, 0).start()
    for o in range(1, SX):
        to = lax.rem(x + o, SX)
        for q in range(SY):
            remote(
                part_ref.at[:, strip(q, to)], gath.at[me, x, :, local(q)],
                asend.at[o - 1], arecv.at[o - 1], x_mate(o),
            ).start()
        remote(
            focus, gath.at[me, x, :, pl.ds(LOCAL, 128)],
            asend.at[o - 1], arecv.at[o - 1], x_mate(o),
        ).start()
    core_copy(0, 0).start()
    pltpu.make_async_copy(refs, refs, refs_sem).wait()

    def tables_and_shifts(q, _):
        at = local(q)
        pixel = lax.broadcasted_iota(jnp.int32, (8, OUT), 1) + (q * ROW + x * OUT)
        fx = (lax.shift_right_logical(pixel, 6) - 64).astype(F32)
        fy = (pixel & 63).astype(F32)
        tab[0, :, at] = (fx * fx + fy * fy) * (INV_TWO_PI / 4096.0)
        tab[7, :, at] = jnp.broadcast_to(noise_ref[:, strip(q, x)], (8, OUT))
        trig = []
        for turns in (fx * (1.0 / 64.0), fy * (1.0 / 64.0), (fx + fy) * (1.0 / 64.0)):
            trig.append((sin_turns(turns + 0.25), sin_turns(turns)))
        for t, (cos, sin) in enumerate(trig):
            tab[1 + 2 * t, :, at] = cos
            tab[2 + 2 * t, :, at] = sin
        for half in range(REFS // 16):
            rows = slice(16 * half, 16 * half + 16)
            real, imag = refs[0, rows, at], refs[1, rows, at]
            shf[0, rows, at] = real
            shf[1, rows, at] = imag
            real, imag = real.astype(F32), imag.astype(F32)
            power = (real * real + imag * imag).astype(BF16) * BF16(-0.5)
            for t in range(TRANS):
                to = slice(t * REFS + 16 * half, t * REFS + 16 * half + 16)
                shf[2, to, at] = power
                if t:
                    cos, sin = twice(trig[t - 1][0]), twice(trig[t - 1][1])
                    shf[0, to, at] = (real * cos - imag * sin).astype(BF16)
                    shf[1, to, at] = (real * sin + imag * cos).astype(BF16)
        return 0

    lax.fori_loop(0, SY, tables_and_shifts, 0)

    def first_hop(o, _):
        swap_landed(o)
        ring_copy(0, 0, o).start()
        ring_copy(1, 0, o).start()
        core_copy(0, o).start()
        return 0

    lax.fori_loop(1, SX, first_hop, 0)

    def weigh(dist, o):
        core_landed(dist, o)
        block, src = lax.rem(z + dist, SZ), source(o)
        rows = pl.ds(pl.multiple_of(block * 64 + src * 16, 16), 16)
        tail = pl.ds(LOCAL, 128)
        d0 = gath[2 * block, src, :, tail].astype(F32)[:8]
        d1 = gath[2 * block + 1, src, :, tail].astype(F32)[:8]
        d = jnp.concatenate([d0, d1], axis=0)
        d = jnp.concatenate([d] * (PART // 128), axis=1)

        def part(k, _):
            at = pl.ds(pl.multiple_of(k * PART, PART), PART)
            transfer = sin_turns(twice(tab[0, :, at]) * d + PHASE) * (-AMP)
            fac = transfer * twice(tab[7, :, at])
            wgt[2, rows, at] = (fac * transfer).astype(BF16)
            a = gath[2 * block, src, :, at].astype(F32)
            b = gath[2 * block + 1, src, :, at].astype(F32)
            for comp in range(2):
                pick = slice(8 * comp, 8 * comp + 8)
                both = jnp.concatenate([a[pick], b[pick]], axis=0)
                wgt[comp, rows, at] = (both * fac).astype(BF16)
            return 0

        lax.fori_loop(0, LOCAL // PART, part, 0)

    def terms(dist):
        block = lax.rem(z + dist, SZ)
        rows = pl.ds(pl.multiple_of(block * 64, 64), 64)
        score[x, block] = (
            nt_dot(wgt[0, rows], shf[0]) + nt_dot(wgt[1, rows], shf[1])
            + nt_dot(wgt[2, rows], shf[2])
        )
        for o in range(1, SX):
            term_copy(dist, o).start()

    def own(o, _):
        weigh(0, o)
        return 0

    def event(e, _):
        step, o = e // SX, lax.rem(e, SX)
        for s in range(SZ // 2):

            @pl.when(step == s)
            def _():
                if s < 3:
                    for way in range(2):
                        ring_landed(way, s, o)
                    if s < 2:
                        for way in range(2):
                            ring_copy(way, s + 1, o).start()
                    else:

                        @pl.when(o < HALF)
                        def _():
                            ring_copy(0, 3, o).start()

                        @pl.when(o >= HALF)
                        def _():
                            ring_copy(1, 3, o).start()

                    core_copy(SZ - 1 - s, o).start()
                    core_copy(s + 1, o).start()
                else:

                    @pl.when(o < HALF)
                    def _():
                        ring_landed(0, 3, o)

                    @pl.when(o >= HALF)
                    def _():
                        ring_landed(1, 3, o)

                    core_copy(4, o).start()

        return 0

    def work(e):
        step, o = e // SX, lax.rem(e, SX)
        ways = 2 - step // 3

        def chunk(way, _):
            weigh((1 - way) * (SZ - 1 - step) + way * (step + 1), o)
            return 0

        lax.fori_loop(0, ways, chunk, 0)

        @pl.when(o == SX - 1)
        def _():
            def block(way, _):
                terms((1 - way) * (SZ - 1 - step) + way * (step + 1))
                return 0

            lax.fori_loop(0, ways, block, 0)

    def turn(e, _):
        event(e, None)

        @pl.when(e > 0)
        def _():
            work(e - 1)

        @pl.when(e == 0)
        def _():
            lax.fori_loop(0, SX, own, 0)
            terms(0)

        return 0

    lax.fori_loop(0, 4 * SX, turn, 0)
    work(4 * SX - 1)

    for dist in range(SZ):
        for o in range(1, SX):
            term_landed(dist, o)
    tops, totals = [], []
    for i in range(SZ // 2):
        rows = [
            (score[0, k] + score[1, k]) + (score[2, k] + score[3, k])
            for k in (2 * i, 2 * i + 1)
        ]
        turned = jnp.concatenate(rows, axis=0).T
        flip[:, i * 128 : (i + 1) * 128] = turned
        top = jnp.max(turned, axis=0, keepdims=True)
        tops.append(top)
        totals.append(jnp.sum(jnp.exp(turned - top), axis=0, keepdims=True))
    stat[me] = jnp.concatenate(tops + totals, axis=0)
    for step in range(1, 2 * SZ):
        stat_copy(step).start()
    for step in range(1, 2 * SZ):
        stat_landed(step)
    stats = stat[...]
    tops, totals = stats[:, 0:4], stats[:, 4:8]
    all_top = jnp.max(tops, axis=0)
    all_total = jnp.sum(totals * jnp.exp(tops - all_top[None]), axis=0)
    log_norm = all_top + jnp.log(all_total)
    for i in range(SZ // 2):
        at = slice(i * 128, (i + 1) * 128)
        posterior = jnp.exp(flip[:, at] - log_norm[i : i + 1]).astype(BF16)
        post[:, at] = posterior
        p = posterior.astype(F32)
        occ[:, at] = (
            p[0:REFS] + p[REFS : 2 * REFS] + p[2 * REFS : 3 * REFS] + p[3 * REFS :]
        ).astype(BF16)

    def y_step(i):
        return 4 + (1 - 2 * lax.rem(i, 2)) * ((i + 1) // 2)

    def y_copy(i):
        return remote(ysend.at[i], yrecv.at[i], ys_sem.at[i], yr_sem.at[i], y_mate(y_step(i)))

    def sums(i):
        at = local(lax.rem(y + y_step(i), SY))
        a0 = jnp.dot(post[...], wgt[0, :, at], preferred_element_type=F32)
        a1 = jnp.dot(post[...], wgt[1, :, at], preferred_element_type=F32)
        ctf = jnp.dot(occ[...], wgt[2, :, at], preferred_element_type=F32)
        real, imag = a0[0:REFS], a1[0:REFS]
        for t in range(1, TRANS):
            cos, sin = tab[2 * t - 1, :, at], tab[2 * t, :, at]
            cos = jnp.concatenate([cos] * (REFS // 8), axis=0)
            sin = jnp.concatenate([sin] * (REFS // 8), axis=0)
            b0, b1 = a0[t * REFS : (t + 1) * REFS], a1[t * REFS : (t + 1) * REFS]
            real = real + b0 * cos + b1 * sin
            imag = imag + b1 * cos - b0 * sin
        return real, imag, ctf

    def piece(i, _):
        real, imag, ctf = sums(i)

        @pl.when(i < SY - 1)
        def _():
            ysend[i, 0:REFS] = real.astype(BF16)
            ysend[i, REFS : 2 * REFS] = imag.astype(BF16)
            ysend[i, 2 * REFS :] = ctf.astype(BF16)
            y_copy(i).start()

        @pl.when(i == SY - 1)
        def _():
            total[0:REFS] = real
            total[REFS : 2 * REFS] = imag
            total[2 * REFS :] = ctf

        return 0

    lax.fori_loop(0, SY, piece, 0)

    def collect(i, _):
        y_copy(i).wait_recv()
        total[...] += yrecv[i].astype(F32)
        return 0

    lax.fori_loop(0, SY - 1, collect, 0)
    weight = total[2 * REFS :] + REGULARIZER
    out_ref[0] = total[0:REFS] / weight
    out_ref[1] = total[REFS : 2 * REFS] / weight

    def drain_ring(o, _):
        for s in range(3):
            for way in range(2):
                ring_copy(way, s, o).wait_send()

        @pl.when(o < HALF)
        def _():
            ring_copy(0, 3, o).wait_send()

        @pl.when(o >= HALF)
        def _():
            ring_copy(1, 3, o).wait_send()

        return 0

    lax.fori_loop(0, SX, drain_ring, 0)

    def drain_blocks(dist, _):
        for o in range(SX):
            core_copy(dist, o).wait_send()
        for o in range(1, SX):
            term_copy(dist, o).wait_send()
        return 0

    lax.fori_loop(0, SZ, drain_blocks, 0)

    def drain_swap(o, _):
        ref = gath.at[me, source(o)]
        remote(ref, ref, asend.at[o - 1], arecv.at[o - 1], x_mate(o)).wait_send()
        return 0

    lax.fori_loop(1, SX, drain_swap, 0)

    def drain_stats(step, _):
        stat_copy(step).wait_send()
        return 0

    lax.fori_loop(1, 2 * SZ, drain_stats, 0)

    def drain_sums(i, _):
        y_copy(i).wait_send()
        return 0

    lax.fori_loop(0, SY - 1, drain_sums, 0)


def shards(particles, defocus, references, noise_weights):
    dma = pltpu.SemaphoreType.DMA
    nblock = 2 * SZ
    rows = particles.shape[0] * particles.shape[1]
    vmem = pl.BlockSpec(memory_space=pltpu.VMEM)
    hbm = pl.BlockSpec(memory_space=pl.ANY)
    return pl.pallas_call(
        kernel,
        out_shape=jax.ShapeDtypeStruct((2, REFS, OUT), F32),
        in_specs=[hbm, vmem, hbm, vmem],
        out_specs=vmem,
        scratch_shapes=[
            pltpu.VMEM((nblock, SX, rows, WIDE), BF16),
            pltpu.VMEM((rows, 128), BF16),
            pltpu.VMEM((2, REFS, LOCAL), BF16),
            pltpu.VMEM((8, 8, LOCAL), F32),
            pltpu.VMEM((3, NPART, LOCAL), BF16),
            pltpu.VMEM((3, NREF, LOCAL), BF16),
            pltpu.VMEM((SX, SZ, 64, NREF), F32),
            pltpu.VMEM((nblock, 8, 128), F32),
            pltpu.VMEM((NREF, NPART), F32),
            pltpu.VMEM((NREF, NPART), BF16),
            pltpu.VMEM((REFS, NPART), BF16),
            pltpu.VMEM((SY - 1, 3 * REFS, OUT), BF16),
            pltpu.VMEM((SY - 1, 3 * REFS, OUT), BF16),
            pltpu.VMEM((3 * REFS, OUT), F32),
            dma,
            dma,
            dma((SX - 1,)),
            dma((SX - 1,)),
            dma((2, 4, SX)),
            dma((2, 4, SX)),
            dma((SZ, SX)),
            dma((SZ, SX)),
            dma((SZ, SX - 1)),
            dma((SZ, SX - 1)),
            dma((nblock - 1,)),
            dma((nblock - 1,)),
            dma((SY - 1,)),
            dma((SY - 1,)),
        ],
        name="expectation",
        compiler_params=pltpu.CompilerParams(
            collective_id=0, has_side_effects=True, vmem_limit_bytes=56 * 2**20
        ),
    )(
        particles.reshape(rows, PIX),
        defocus.reshape(1, 8),
        references,
        noise_weights.reshape(1, PIX),
    )


def solution(mesh):
    return jax.shard_map(
        shards,
        mesh=mesh,
        in_specs=(P(None, ("dom", "ref"), None), P(("dom", "ref")), P(None, "ref", None), P()),
        out_specs=P(None, "ref", "dom"),
        check_vma=False,
    )
```

time: 618 us -> 70.6 us (0.11)
  the two profiles are of different devices: /device:TPU:16 before, /device:TPU:1 now
where the time goes in v2:
time: 70.6 us; the launch traced here: 70.3 us
  Pallas kernels  68.8 us (97%)
  local copies, waits for them, and re-layouts  1.47 us (2%)
    pallas_call x1, Pallas kernels, shards(): pl.pallas_call(kernel, out_shape=jax.ShapeDtypeStruct((2, REFS, OUT), F32...  68.8 us
    unnamed x1, local copies, waits for them, and re-layouts  1.47 us

profile of v2, /device:TPU:1, one launch (start us, length us, event | category | flops | bytes accessed | tf_op | source)
XLA Modules:
  0.0 70.3 jit_solution(15905785282265839462)
XLA Ops:
  0.0 68.8 %expectation.1 = f32[2,32,256]{2,1,0:T(8,128)} custom-call(bf16[16,8192]{1,0:T(8,128)(2,1)} %bitcast.3, bf16[1,8]{1,0:T(2,128)(2,1)} %bitcast.5, bf16[2,32,8192]{2,1,0:T(8,128)(2,1)} %refs_ref.1, f32[1,8192]{1,0:T(1,128)} %bitcast.4), custom_call_target="tpu_custom_call" | custom-call | tf_op jit(solution)/shard_map/expectation/pallas_call | solution.py:468
  68.8 1.5 %copy.6 = f32[2,32,256]{2,1,0:T(8,128)} copy(f32[2,32,256]{2,1,0:T(8,128)} %expectation.1) | data formatting | bytes 131072

commit v3 on v2

--- a/solution.py
+++ b/solution.py
@@ -15,6 +15,7 @@
 WIDE = LOCAL + 128
 PART = 512
 HALF = SX // 2
+HALFZ = SZ // 2
 NREF = TRANS * REFS
 NPART = SZ * SX * 16
 REGULARIZER = 0.05
@@ -45,6 +46,10 @@
     return acc * v
 
 
+def hop(o):
+    return o + (o // 2) * (5 - 2 * o)
+
+
 def nt_dot(a, b):
     return lax.dot_general(a, b, (((1,), (1,)), ((), ())), preferred_element_type=F32)
 
@@ -55,9 +60,9 @@
 
 def kernel(
     part_ref, focus_ref, refs_ref, noise_ref, out_ref,
-    gath, focus, refs, tab, wgt, shf, score, stat, flip, post, occ, ysend, yrecv, total,
-    local_sem, refs_sem, asend, arecv, ring_send, ring_recv, core_send, core_recv,
-    tsend, trecv, ssend, srecv, ys_sem, yr_sem,
+    gath, focus, few, refs, noise, tab, wgt, shf, score, stat, flip, post, occ, ysend, yrecv, total,
+    local_sem, refs_sem, noise_sem, focus_sem, asend, arecv, ring_send, ring_recv, core_send, core_recv,
+    tsend, trecv, lsend, lrecv, ssend, srecv, ys_sem, yr_sem,
 ):
     dom, me = lax.axis_index("dom"), lax.axis_index("ref")
     y, x, z, c = dom // SX, dom % SX, me // 2, me % 2
@@ -80,21 +85,13 @@
         return (lax.rem(y + step, SY) * SX + x, me)
 
     def source(o):
-        return lax.rem(x + SX - o, SX)
+        return lax.rem(x + SX - hop(o), SX)
 
     def strip(q, to):
         return pl.ds(pl.multiple_of(q * ROW + to * OUT, OUT), OUT)
 
     def local(q):
         return pl.ds(pl.multiple_of(q * OUT, OUT), OUT)
-
-    barrier = pltpu.get_barrier_semaphore()
-    for step in range(1, 2 * SZ):
-        pl.semaphore_signal(barrier, inc=1, device_id=mate(step), device_id_type=MESH)
-    for step in range(1, SX):
-        pl.semaphore_signal(barrier, inc=1, device_id=x_mate(step), device_id_type=MESH)
-    for step in range(1, SY):
-        pl.semaphore_signal(barrier, inc=1, device_id=y_mate(step), device_id_type=MESH)
 
     for q in range(SY):
         pltpu.make_async_copy(
@@ -104,10 +101,24 @@
         pltpu.make_async_copy(
             refs_ref.at[:, :, strip(q, x)], refs.at[:, :, local(q)], refs_sem
         ).start()
+    for q in range(SY):
+        pltpu.make_async_copy(
+            noise_ref.at[:, strip(q, x)], noise.at[:, local(q)], noise_sem
+        ).start()
+    seen = pltpu.make_async_copy(focus_ref, few, focus_sem)
+    seen.start()
+    barrier = pltpu.get_barrier_semaphore()
+    for step in range(1, 2 * SZ):
+        pl.semaphore_signal(barrier, inc=1, device_id=mate(step), device_id_type=MESH)
+    for step in range(1, SX):
+        pl.semaphore_signal(barrier, inc=1, device_id=x_mate(step), device_id_type=MESH)
+    for step in range(1, SY):
+        pl.semaphore_signal(barrier, inc=1, device_id=y_mate(step), device_id_type=MESH)
+    seen.wait()
     diagonal = lax.broadcasted_iota(jnp.int32, (8, 8), 0) == lax.broadcasted_iota(
         jnp.int32, (8, 8), 1
     )
-    wide = jnp.broadcast_to(focus_ref[...].astype(F32), (8, 8))
+    wide = jnp.broadcast_to(few[...].astype(F32), (8, 8))
     column = jnp.sum(jnp.where(diagonal, wide, 0.0), axis=1, keepdims=True)
     spread = twice(jnp.broadcast_to(column, (8, 128))).astype(BF16)
     focus[...] = spread
@@ -142,15 +153,26 @@
 
     def swap_landed(o):
         ref = gath.at[me, source(o)]
-        remote(ref, ref, asend.at[o - 1], arecv.at[o - 1], x_mate(o)).wait_recv()
+        remote(ref, ref, asend.at[o - 1], arecv.at[o - 1], x_mate(hop(o))).wait_recv()
 
     def term_copy(dist, o):
         ref = score.at[x, lax.rem(z + dist, SZ)]
-        return remote(ref, ref, tsend.at[dist, o - 1], trecv.at[dist, o - 1], x_mate(o))
+        return remote(ref, ref, tsend.at[dist, o - 1], trecv.at[dist, o - 1], x_mate(hop(o)))
 
     def term_landed(dist, o):
         ref = score.at[source(o), lax.rem(z + dist, SZ)]
-        remote(ref, ref, tsend.at[dist, o - 1], trecv.at[dist, o - 1], x_mate(o)).wait_recv()
+        remote(ref, ref, tsend.at[dist, o - 1], trecv.at[dist, o - 1], x_mate(hop(o))).wait_recv()
+
+    def last_copy(u, o):
+        at = pl.ds(pl.multiple_of(source(u) * 16, 16), 16)
+        ref = score.at[x, lax.rem(z + HALFZ, SZ), at]
+        return remote(ref, ref, lsend.at[u, o - 1], lrecv.at[u, o - 1], x_mate(hop(o)))
+
+    def last_landed(u, o):
+        row = lax.rem(source(o) + SX - hop(u), SX)
+        at = pl.ds(pl.multiple_of(row * 16, 16), 16)
+        ref = score.at[source(o), lax.rem(z + HALFZ, SZ), at]
+        remote(ref, ref, lsend.at[u, o - 1], lrecv.at[u, o - 1], x_mate(hop(o))).wait_recv()
 
     def stat_copy(step):
         return remote(
@@ -164,18 +186,17 @@
     ring_copy(0, 0, 0).start()
     ring_copy(1, 0, 0).start()
     for o in range(1, SX):
-        to = lax.rem(x + o, SX)
+        to = lax.rem(x + hop(o), SX)
         for q in range(SY):
             remote(
                 part_ref.at[:, strip(q, to)], gath.at[me, x, :, local(q)],
-                asend.at[o - 1], arecv.at[o - 1], x_mate(o),
+                asend.at[o - 1], arecv.at[o - 1], x_mate(hop(o)),
             ).start()
         remote(
             focus, gath.at[me, x, :, pl.ds(LOCAL, 128)],
-            asend.at[o - 1], arecv.at[o - 1], x_mate(o),
+            asend.at[o - 1], arecv.at[o - 1], x_mate(hop(o)),
         ).start()
     core_copy(0, 0).start()
-    pltpu.make_async_copy(refs, refs, refs_sem).wait()
 
     def tables_and_shifts(q, _):
         at = local(q)
@@ -183,7 +204,7 @@
         fx = (lax.shift_right_logical(pixel, 6) - 64).astype(F32)
         fy = (pixel & 63).astype(F32)
         tab[0, :, at] = (fx * fx + fy * fy) * (INV_TWO_PI / 4096.0)
-        tab[7, :, at] = jnp.broadcast_to(noise_ref[:, strip(q, x)], (8, OUT))
+        tab[7, :, at] = jnp.broadcast_to(noise[:, at], (8, OUT))
         trig = []
         for turns in (fx * (1.0 / 64.0), fy * (1.0 / 64.0), (fx + fy) * (1.0 / 64.0)):
             trig.append((sin_turns(turns + 0.25), sin_turns(turns)))
@@ -206,16 +227,12 @@
                     shf[1, to, at] = (real * sin + imag * cos).astype(BF16)
         return 0
 
-    lax.fori_loop(0, SY, tables_and_shifts, 0)
-
     def first_hop(o, _):
         swap_landed(o)
         ring_copy(0, 0, o).start()
         ring_copy(1, 0, o).start()
         core_copy(0, o).start()
         return 0
-
-    lax.fori_loop(1, SX, first_hop, 0)
 
     def weigh(dist, o):
         core_landed(dist, o)
@@ -242,22 +259,34 @@
 
         lax.fori_loop(0, LOCAL // PART, part, 0)
 
-    def terms(dist):
-        block = lax.rem(z + dist, SZ)
-        rows = pl.ds(pl.multiple_of(block * 64, 64), 64)
-        score[x, block] = (
+    def dots(rows):
+        return (
             nt_dot(wgt[0, rows], shf[0]) + nt_dot(wgt[1, rows], shf[1])
             + nt_dot(wgt[2, rows], shf[2])
         )
+
+    def terms(dist):
+        block = lax.rem(z + dist, SZ)
+        score[x, block] = dots(pl.ds(pl.multiple_of(block * 64, 64), 64))
         for o in range(1, SX):
             term_copy(dist, o).start()
 
+    def last_terms(u):
+        at, block = pl.ds(pl.multiple_of(source(u) * 16, 16), 16), lax.rem(z + HALFZ, SZ)
+        score[x, block, at] = dots(pl.ds(pl.multiple_of(block * 64 + source(u) * 16, 16), 16))
+        for o in range(1, SX):
+            last_copy(u, o).start()
+
     def own(o, _):
         weigh(0, o)
         return 0
 
+    def chunk_of(e):
+        k, last = lax.rem(e, SX), e // (3 * SX)
+        return k + last * (lax.rem(k, HALF) * HALF + k // HALF - k)
+
     def event(e, _):
-        step, o = e // SX, lax.rem(e, SX)
+        step, o = e // SX, chunk_of(e)
         for s in range(SZ // 2):
 
             @pl.when(step == s)
@@ -295,7 +324,7 @@
         return 0
 
     def work(e):
-        step, o = e // SX, lax.rem(e, SX)
+        step, o = e // SX, chunk_of(e)
         ways = 2 - step // 3
 
         def chunk(way, _):
@@ -304,7 +333,11 @@
 
         lax.fori_loop(0, ways, chunk, 0)
 
-        @pl.when(o == SX - 1)
+        @pl.when(step == 3)
+        def _():
+            last_terms(o)
+
+        @pl.when((step < 3) & (o == SX - 1))
         def _():
             def block(way, _):
                 terms((1 - way) * (SZ - 1 - step) + way * (step + 1))
@@ -314,24 +347,26 @@
 
     def turn(e, _):
         event(e, None)
-
-        @pl.when(e > 0)
-        def _():
-            work(e - 1)
-
-        @pl.when(e == 0)
-        def _():
-            lax.fori_loop(0, SX, own, 0)
-            terms(0)
-
-        return 0
-
-    lax.fori_loop(0, 4 * SX, turn, 0)
+        work(e - 1)
+        return 0
+
+    event(0, None)
+    lax.fori_loop(1, SX, first_hop, 0)
+    pltpu.make_async_copy(refs, refs, refs_sem).wait()
+    pltpu.make_async_copy(noise, noise, noise_sem).wait()
+    lax.fori_loop(0, SY, tables_and_shifts, 0)
+    lax.fori_loop(0, SX, own, 0)
+    terms(0)
+    lax.fori_loop(1, 4 * SX, turn, 0)
     work(4 * SX - 1)
 
     for dist in range(SZ):
+        if dist != HALFZ:
+            for o in range(1, SX):
+                term_landed(dist, o)
+    for u in range(SX):
         for o in range(1, SX):
-            term_landed(dist, o)
+            last_landed(u, o)
     tops, totals = [], []
     for i in range(SZ // 2):
         rows = [
@@ -344,7 +379,7 @@
         tops.append(top)
         totals.append(jnp.sum(jnp.exp(turned - top), axis=0, keepdims=True))
     stat[me] = jnp.concatenate(tops + totals, axis=0)
-    for step in range(1, 2 * SZ):
+    for step in sorted(range(1, 2 * SZ), key=lambda k: abs(k - SZ)):
         stat_copy(step).start()
     for step in range(1, 2 * SZ):
         stat_landed(step)
@@ -433,15 +468,26 @@
     def drain_blocks(dist, _):
         for o in range(SX):
             core_copy(dist, o).wait_send()
+
+        @pl.when(dist != HALFZ)
+        def _():
+            for o in range(1, SX):
+                term_copy(dist, o).wait_send()
+
+        return 0
+
+    lax.fori_loop(0, SZ, drain_blocks, 0)
+
+    def drain_last(u, _):
         for o in range(1, SX):
-            term_copy(dist, o).wait_send()
-        return 0
-
-    lax.fori_loop(0, SZ, drain_blocks, 0)
+            last_copy(u, o).wait_send()
+        return 0
+
+    lax.fori_loop(0, SX, drain_last, 0)
 
     def drain_swap(o, _):
         ref = gath.at[me, source(o)]
-        remote(ref, ref, asend.at[o - 1], arecv.at[o - 1], x_mate(o)).wait_send()
+        remote(ref, ref, asend.at[o - 1], arecv.at[o - 1], x_mate(hop(o))).wait_send()
         return 0
 
     lax.fori_loop(1, SX, drain_swap, 0)
@@ -467,13 +513,15 @@
     hbm = pl.BlockSpec(memory_space=pl.ANY)
     return pl.pallas_call(
         kernel,
-        out_shape=jax.ShapeDtypeStruct((2, REFS, OUT), F32),
-        in_specs=[hbm, vmem, hbm, vmem],
+        out_shape=pltpu.VMEM((2, REFS, OUT), F32),
+        in_specs=[hbm, hbm, hbm, hbm],
         out_specs=vmem,
         scratch_shapes=[
             pltpu.VMEM((nblock, SX, rows, WIDE), BF16),
             pltpu.VMEM((rows, 128), BF16),
+            pltpu.VMEM((1, 8), BF16),
             pltpu.VMEM((2, REFS, LOCAL), BF16),
+            pltpu.VMEM((1, LOCAL), F32),
             pltpu.VMEM((8, 8, LOCAL), F32),
             pltpu.VMEM((3, NPART, LOCAL), BF16),
             pltpu.VMEM((3, NREF, LOCAL), BF16),
@@ -487,6 +535,8 @@
             pltpu.VMEM((3 * REFS, OUT), F32),
             dma,
             dma,
+            dma,
+            dma,
             dma((SX - 1,)),
             dma((SX - 1,)),
             dma((2, 4, SX)),
@@ -495,6 +545,8 @@
             dma((SZ, SX)),
             dma((SZ, SX - 1)),
             dma((SZ, SX - 1)),
+            dma((SX, SX - 1)),
+            dma((SX, SX - 1)),
             dma((nblock - 1,)),
             dma((nblock - 1,)),
             dma((SY - 1,)),

time: 70.6 us -> 67.8 us (0.960)
  Pallas kernels: 68.8 us -> 67 us
  local copies, waits for them, and re-layouts: 1.47 us -> 0.63 us
    pallas_call x1, Pallas kernels: 68.8 us -> 67 us  [shards(): pl.pallas_call(kernel, out_shape=pltpu.VMEM((2, REFS, OUT), F32), in_spec...]
    unnamed x1, local copies, waits for them, and re-layouts: 1.47 us -> 0.63 us
where the time goes in v3:
time: 67.8 us; the launch traced here: 67.6 us
  Pallas kernels  67 us (99%)
    pallas_call x1, Pallas kernels, shards(): pl.pallas_call(kernel, out_shape=pltpu.VMEM((2, REFS, OUT), F32), in_spec...  67 us

profile of v3, /device:TPU:1, one launch (start us, length us, event | category | flops | bytes accessed | tf_op | source)
XLA Modules:
  0.0 67.6 jit_solution(3364061345471878685)
XLA Ops:
  0.0 67.0 %expectation.1 = f32[2,32,256]{2,1,0:T(8,128)S(1)} custom-call(bf16[16,8192]{1,0:T(8,128)(2,1)} %bitcast.3, bf16[1,8]{1,0:T(2,128)(2,1)} %bitcast.5, bf16[2,32,8192]{2,1,0:T(8,128)(2,1)} %refs_ref.1, f32[1,8192]{1,0:T(1,128)} %bitcast.4), custom_call_target="tpu_custom_call" | custom-call | tf_op jit(solution)/shard_map/expectation/pallas_call | solution.py:514
  67.0 0.6 copy.6

commit v4 on v3

--- a/solution.py
+++ b/solution.py
@@ -17,6 +17,7 @@
 HALF = SX // 2
 HALFZ = SZ // 2
 NREF = TRANS * REFS
+MID = 3 * REFS // 2
 NPART = SZ * SX * 16
 REGULARIZER = 0.05
 
@@ -60,7 +61,7 @@
 
 def kernel(
     part_ref, focus_ref, refs_ref, noise_ref, out_ref,
-    gath, focus, few, refs, noise, tab, wgt, shf, score, stat, flip, post, occ, ysend, yrecv, total,
+    gath, focus, few, refs, noise, tab, wgt, shf, score, stat, flip, post, occ, ysend, yrecv, hold, total,
     local_sem, refs_sem, noise_sem, focus_sem, asend, arecv, ring_send, ring_recv, core_send, core_recv,
     tsend, trecv, lsend, lrecv, ssend, srecv, ys_sem, yr_sem,
 ):
@@ -398,10 +399,22 @@
         ).astype(BF16)
 
     def y_step(i):
-        return 4 + (1 - 2 * lax.rem(i, 2)) * ((i + 1) // 2)
-
-    def y_copy(i):
-        return remote(ysend.at[i], yrecv.at[i], ys_sem.at[i], yr_sem.at[i], y_mate(y_step(i)))
+        j = (i + 1) // 2
+        return 4 - j + 2 * j * lax.rem(i + 1, 2)
+
+    top_half, low_half = slice(0, MID), slice(MID, 2 * MID)
+
+    def y_copy(i, step, rows=slice(0, 2 * MID), sem=None):
+        sem = i if sem is None else sem
+        return remote(
+            ysend.at[i, rows], yrecv.at[i, rows], ys_sem.at[sem], yr_sem.at[sem], y_mate(step)
+        )
+
+    def y_copies():
+        return (
+            y_copy(0, 2, top_half), y_copy(1, 1), y_copy(2, SY - 1), y_copy(3, 2),
+            y_copy(4, SY - 2), y_copy(5, 1), y_copy(6, SY - 1), y_copy(0, SY - 2, low_half, 7),
+        )
 
     def sums(i):
         at = local(lax.rem(y + y_step(i), SY))
@@ -421,12 +434,17 @@
     def piece(i, _):
         real, imag, ctf = sums(i)
 
-        @pl.when(i < SY - 1)
+        @pl.when((i < 3) | (i == 5) | (i == 6))
         def _():
             ysend[i, 0:REFS] = real.astype(BF16)
             ysend[i, REFS : 2 * REFS] = imag.astype(BF16)
             ysend[i, 2 * REFS :] = ctf.astype(BF16)
-            y_copy(i).start()
+
+        @pl.when((i == 3) | (i == 4))
+        def _():
+            hold[i - 3, 0:REFS] = real
+            hold[i - 3, REFS : 2 * REFS] = imag
+            hold[i - 3, 2 * REFS :] = ctf
 
         @pl.when(i == SY - 1)
         def _():
@@ -434,16 +452,39 @@
             total[REFS : 2 * REFS] = imag
             total[2 * REFS :] = ctf
 
+        for k in (0, 1, 2, 5, 6):
+
+            @pl.when(i == k)
+            def _():
+                y_copies()[k].start()
+                if k == 0:
+                    y_copies()[7].start()
+
         return 0
 
     lax.fori_loop(0, SY, piece, 0)
 
-    def collect(i, _):
-        y_copy(i).wait_recv()
-        total[...] += yrecv[i].astype(F32)
-        return 0
-
-    lax.fori_loop(0, SY - 1, collect, 0)
+    near, far = y_copies()[1], y_copies()[0]
+    near.wait_recv()
+    far.wait_recv()
+    both = hold[0] + yrecv[1].astype(F32)
+    ysend[3, top_half] = (both[top_half] + yrecv[0, top_half].astype(F32)).astype(BF16)
+    ysend[3, low_half] = both[low_half].astype(BF16)
+    y_copies()[3].start()
+    near, far = y_copies()[2], y_copies()[7]
+    near.wait_recv()
+    far.wait_recv()
+    both = hold[1] + yrecv[2].astype(F32)
+    ysend[4, top_half] = both[top_half].astype(BF16)
+    ysend[4, low_half] = (both[low_half] + yrecv[0, low_half].astype(F32)).astype(BF16)
+    y_copies()[4].start()
+
+    y_copies()[5].wait_recv()
+    y_copies()[6].wait_recv()
+    total[...] += yrecv[5].astype(F32) + yrecv[6].astype(F32)
+    y_copies()[3].wait_recv()
+    y_copies()[4].wait_recv()
+    total[...] += yrecv[3].astype(F32) + yrecv[4].astype(F32)
     weight = total[2 * REFS :] + REGULARIZER
     out_ref[0] = total[0:REFS] / weight
     out_ref[1] = total[REFS : 2 * REFS] / weight
@@ -498,11 +539,8 @@
 
     lax.fori_loop(1, 2 * SZ, drain_stats, 0)
 
-    def drain_sums(i, _):
-        y_copy(i).wait_send()
-        return 0
-
-    lax.fori_loop(0, SY - 1, drain_sums, 0)
+    for copy in y_copies():
+        copy.wait_send()
 
 
 def shards(particles, defocus, references, noise_weights):
@@ -532,6 +570,7 @@
             pltpu.VMEM((REFS, NPART), BF16),
             pltpu.VMEM((SY - 1, 3 * REFS, OUT), BF16),
             pltpu.VMEM((SY - 1, 3 * REFS, OUT), BF16),
+            pltpu.VMEM((2, 3 * REFS, OUT), F32),
             pltpu.VMEM((3 * REFS, OUT), F32),
             dma,
             dma,
@@ -549,8 +588,8 @@
             dma((SX, SX - 1)),
             dma((nblock - 1,)),
             dma((nblock - 1,)),
-            dma((SY - 1,)),
-            dma((SY - 1,)),
+            dma((SY,)),
+            dma((SY,)),
         ],
         name="expectation",
         compiler_params=pltpu.CompilerParams(

time: 67.8 us -> 65.5 us (0.966); the launches traced: 67.6 us -> 64.2 us
  Pallas kernels: 67 us -> 63.6 us
    pallas_call x1, Pallas kernels: 67 us -> 63.6 us  [shards(): pl.pallas_call(kernel, out_shape=pltpu.VMEM((2, REFS, OUT), F32), in_spec...]
where the time goes in v4:
time: 65.5 us; the launch traced here: 64.2 us
  Pallas kernels  63.6 us (97%)
    pallas_call x1, Pallas kernels, shards(): pl.pallas_call(kernel, out_shape=pltpu.VMEM((2, REFS, OUT), F32), in_spec...  63.6 us

profile of v4, /device:TPU:1, one launch (start us, length us, event | category | flops | bytes accessed | tf_op | source)
XLA Modules:
  0.0 64.2 jit_solution(3906805554222238267)
XLA Ops:
  0.0 63.6 %expectation.1 = f32[2,32,256]{2,1,0:T(8,128)S(1)} custom-call(bf16[16,8192]{1,0:T(8,128)(2,1)} %bitcast.3, bf16[1,8]{1,0:T(2,128)(2,1)} %bitcast.5, bf16[2,32,8192]{2,1,0:T(8,128)(2,1)} %refs_ref.1, f32[1,8192]{1,0:T(1,128)} %bitcast.4), custom_call_target="tpu_custom_call" | custom-call | tf_op jit(solution)/shard_map/expectation/pallas_call | solution.py:552
  63.6 0.6 copy.6

commit v5 on v4

--- a/solution.py
+++ b/solution.py
@@ -51,17 +51,13 @@
     return o + (o // 2) * (5 - 2 * o)
 
 
-def nt_dot(a, b):
-    return lax.dot_general(a, b, (((1,), (1,)), ((), ())), preferred_element_type=F32)
-
-
 def twice(a):
     return jnp.concatenate([a, a], axis=0)
 
 
 def kernel(
     part_ref, focus_ref, refs_ref, noise_ref, out_ref,
-    gath, focus, few, refs, noise, tab, wgt, shf, score, stat, flip, post, occ, ysend, yrecv, hold, total,
+    gath, focus, few, refs, noise, tab, wgt, shf, turned, score, stat, flip, post, occ, ysend, yrecv, hold, total,
     local_sem, refs_sem, noise_sem, focus_sem, asend, arecv, ring_send, ring_recv, core_send, core_recv,
     tsend, trecv, lsend, lrecv, ssend, srecv, ys_sem, yr_sem,
 ):
@@ -94,10 +90,27 @@
     def local(q):
         return pl.ds(pl.multiple_of(q * OUT, OUT), OUT)
 
+    barrier = pltpu.get_barrier_semaphore()
+
+    def greet(device):
+        pl.semaphore_signal(barrier, inc=1, device_id=device, device_id_type=MESH)
+
+    greet(up)
+    greet(down)
+    for step in range(1, SX):
+        greet(x_mate(step))
+    greet(other)
     for q in range(SY):
         pltpu.make_async_copy(
             part_ref.at[:, strip(q, x)], gath.at[me, x, :, local(q)], local_sem
         ).start()
+    for step in range(3, 2 * SZ - 2):
+        greet(mate(step))
+    greet(mate(2 * SZ - 1 - (2 * SZ - 2) * c))
+    for step in range(1, SY):
+        greet(y_mate(step))
+    seen = pltpu.make_async_copy(focus_ref, few, focus_sem)
+    seen.start()
     for q in range(SY):
         pltpu.make_async_copy(
             refs_ref.at[:, :, strip(q, x)], refs.at[:, :, local(q)], refs_sem
@@ -106,15 +119,6 @@
         pltpu.make_async_copy(
             noise_ref.at[:, strip(q, x)], noise.at[:, local(q)], noise_sem
         ).start()
-    seen = pltpu.make_async_copy(focus_ref, few, focus_sem)
-    seen.start()
-    barrier = pltpu.get_barrier_semaphore()
-    for step in range(1, 2 * SZ):
-        pl.semaphore_signal(barrier, inc=1, device_id=mate(step), device_id_type=MESH)
-    for step in range(1, SX):
-        pl.semaphore_signal(barrier, inc=1, device_id=x_mate(step), device_id_type=MESH)
-    for step in range(1, SY):
-        pl.semaphore_signal(barrier, inc=1, device_id=y_mate(step), device_id_type=MESH)
     seen.wait()
     diagonal = lax.broadcasted_iota(jnp.int32, (8, 8), 0) == lax.broadcasted_iota(
         jnp.int32, (8, 8), 1
@@ -226,6 +230,8 @@
                     cos, sin = twice(trig[t - 1][0]), twice(trig[t - 1][1])
                     shf[0, to, at] = (real * cos - imag * sin).astype(BF16)
                     shf[1, to, at] = (real * sin + imag * cos).astype(BF16)
+        for comp in range(3):
+            turned[comp, at] = shf[comp, :, at].T
         return 0
 
     def first_hop(o, _):
@@ -261,10 +267,9 @@
         lax.fori_loop(0, LOCAL // PART, part, 0)
 
     def dots(rows):
-        return (
-            nt_dot(wgt[0, rows], shf[0]) + nt_dot(wgt[1, rows], shf[1])
-            + nt_dot(wgt[2, rows], shf[2])
-        )
+        acc = jnp.dot(wgt[0, rows], turned[0], preferred_element_type=F32)
+        acc = acc + jnp.dot(wgt[1, rows], turned[1], preferred_element_type=F32)
+        return acc + jnp.dot(wgt[2, rows], turned[2], preferred_element_type=F32)
 
     def terms(dist):
         block = lax.rem(z + dist, SZ)
@@ -374,11 +379,12 @@
             (score[0, k] + score[1, k]) + (score[2, k] + score[3, k])
             for k in (2 * i, 2 * i + 1)
         ]
-        turned = jnp.concatenate(rows, axis=0).T
-        flip[:, i * 128 : (i + 1) * 128] = turned
-        top = jnp.max(turned, axis=0, keepdims=True)
+        block = jnp.concatenate(rows, axis=0).T
+        top = jnp.max(block, axis=0, keepdims=True)
         tops.append(top)
-        totals.append(jnp.sum(jnp.exp(turned - top), axis=0, keepdims=True))
+        spread = jnp.exp(block - top)
+        flip[:, i * 128 : (i + 1) * 128] = spread
+        totals.append(jnp.sum(spread, axis=0, keepdims=True))
     stat[me] = jnp.concatenate(tops + totals, axis=0)
     for step in sorted(range(1, 2 * SZ), key=lambda k: abs(k - SZ)):
         stat_copy(step).start()
@@ -388,10 +394,10 @@
     tops, totals = stats[:, 0:4], stats[:, 4:8]
     all_top = jnp.max(tops, axis=0)
     all_total = jnp.sum(totals * jnp.exp(tops - all_top[None]), axis=0)
-    log_norm = all_top + jnp.log(all_total)
+    share = jnp.exp(stat[me, 0:4] - all_top) / all_total
     for i in range(SZ // 2):
         at = slice(i * 128, (i + 1) * 128)
-        posterior = jnp.exp(flip[:, at] - log_norm[i : i + 1]).astype(BF16)
+        posterior = (flip[:, at] * share[i : i + 1]).astype(BF16)
         post[:, at] = posterior
         p = posterior.astype(F32)
         occ[:, at] = (
@@ -563,6 +569,7 @@
             pltpu.VMEM((8, 8, LOCAL), F32),
             pltpu.VMEM((3, NPART, LOCAL), BF16),
             pltpu.VMEM((3, NREF, LOCAL), BF16),
+            pltpu.VMEM((3, LOCAL, NREF), BF16),
             pltpu.VMEM((SX, SZ, 64, NREF), F32),
             pltpu.VMEM((nblock, 8, 128), F32),
             pltpu.VMEM((NREF, NPART), F32),

time: 65.5 us -> 63.9 us (0.976)
  Pallas kernels: 63.6 us -> 62.4 us
    pallas_call x1, Pallas kernels: 63.6 us -> 62.4 us  [shards(): pl.pallas_call(kernel, out_shape=pltpu.VMEM((2, REFS, OUT), F32), in_spec...]
where the time goes in v5:
time: 63.9 us; the launch traced here: 63 us
  Pallas kernels  62.4 us (98%)
    pallas_call x1, Pallas kernels, shards(): pl.pallas_call(kernel, out_shape=pltpu.VMEM((2, REFS, OUT), F32), in_spec...  62.4 us

profile of v5, /device:TPU:1, one launch (start us, length us, event | category | flops | bytes accessed | tf_op | source)
XLA Modules:
  0.0 63.0 jit_solution(1519906133891135555)
XLA Ops:
  0.0 62.4 %expectation.1 = f32[2,32,256]{2,1,0:T(8,128)S(1)} custom-call(bf16[16,8192]{1,0:T(8,128)(2,1)} %bitcast.3, bf16[1,8]{1,0:T(2,128)(2,1)} %bitcast.5, bf16[2,32,8192]{2,1,0:T(8,128)(2,1)} %refs_ref.1, f32[1,8192]{1,0:T(1,128)} %bitcast.4), custom_call_target="tpu_custom_call" | custom-call | tf_op jit(solution)/shard_map/expectation/pallas_call | solution.py:558
  62.4 0.6 %copy.6 = f32[2,32,256]{2,1,0:T(8,128)} copy(f32[2,32,256]{2,1,0:T(8,128)S(1)} %expectation.1) | data formatting | bytes 131072

commit v6 on v5

--- a/solution.py
+++ b/solution.py
@@ -13,7 +13,7 @@
 ROW = SX * OUT
 LOCAL = SY * OUT
 WIDE = LOCAL + 128
-PART = 512
+PART = 1024
 HALF = SX // 2
 HALFZ = SZ // 2
 NREF = TRANS * REFS
@@ -300,10 +300,9 @@
                 if s < 3:
                     for way in range(2):
                         ring_landed(way, s, o)
-                    if s < 2:
-                        for way in range(2):
+                        if s < 2:
                             ring_copy(way, s + 1, o).start()
-                    else:
+                    if s == 2:
 
                         @pl.when(o < HALF)
                         def _():

time: 63.9 us -> 64.1 us (level)
  the two profiles are of different devices: /device:TPU:1 before, /device:TPU:8 now
where the time goes in v6:
time: 64.1 us; the launch traced here: 63.9 us
  Pallas kernels  63.2 us (99%)
    pallas_call x1, Pallas kernels, shards(): pl.pallas_call(kernel, out_shape=pltpu.VMEM((2, REFS, OUT), F32), in_spec...  63.2 us

profile of v6, /device:TPU:8, one launch (start us, length us, event | category | flops | bytes accessed | tf_op | source)
XLA Modules:
  0.0 63.9 jit_solution(12771238747552083793)
XLA Ops:
  0.0 63.2 %expectation.1 = f32[2,32,256]{2,1,0:T(8,128)S(1)} custom-call(bf16[16,8192]{1,0:T(8,128)(2,1)} %bitcast.3, bf16[1,8]{1,0:T(2,128)(2,1)} %bitcast.5, bf16[2,32,8192]{2,1,0:T(8,128)(2,1)} %refs_ref.1, f32[1,8192]{1,0:T(1,128)} %bitcast.4), custom_call_target="tpu_custom_call" | custom-call | tf_op jit(solution)/shard_map/expectation/pallas_call | solution.py:557
  63.2 0.6 copy.6
